TPU v7x, 32 devices: a whole 2x2x4 slice. The times are simulated.
32 devices in a mesh: dp: 4 (over y, x), ctx: 8 (over z, core).
Axes of the slice: x: 2, y: 2, z: 4, core: 2. Of those that a mesh axis runs over, the one named last changes fastest.
Arguments:
- tokens: bfloat16 [1024, 8, 1024], P('ctx', 'dp'), may hold values from -6 to 6
- cotangent: bfloat16 [1024, 8, 1024], P('ctx', 'dp'), may hold values from -6 to 6
- segments: int32 [8, 1024], P('dp'), may hold values from 0 to 8, as said below
- w_qkv: bfloat16 [1024, 3072], P(('dp', 'ctx')), may hold values from -0.1875 to 0.1875
- b_qkv: bfloat16 [3072], P(('dp', 'ctx')), may hold values from -2 to 2
- w_out: bfloat16 [1024, 1024], P(('dp', 'ctx')), may hold values from -0.75 to 0.75
- b_out: bfloat16 [1024], P(('dp', 'ctx')), may hold values from -2 to 2
- w_up: bfloat16 [1024, 4096], P(('dp', 'ctx')), may hold values from -0.1875 to 0.1875
- b_up: bfloat16 [4096], P(('dp', 'ctx')), may hold values from -2 to 2
- w_down: bfloat16 [4096, 1024], P(('dp', 'ctx')), may hold values from -0.09375 to 0.09375
- b_down: bfloat16 [1024], P(('dp', 'ctx')), may hold values from -2 to 2
- norm1_gain: bfloat16 [1024], P(('dp', 'ctx')), may hold values from 0.099609375 to 1.8984375
- norm1_bias: bfloat16 [1024], P(('dp', 'ctx')), may hold values from -2 to 2
- norm2_gain: bfloat16 [1024], P(('dp', 'ctx')), may hold values from 0.099609375 to 1.8984375
- norm2_bias: bfloat16 [1024], P(('dp', 'ctx')), may hold values from -2 to 2
Outputs:
- mixed: bfloat16 [1024, 8, 1024], P('ctx', 'dp')
- tokens_grad: bfloat16 [1024, 8, 1024], P('ctx', 'dp')
- w_qkv_grad: float32 [1024, 3072], P(('dp', 'ctx'))
- b_qkv_grad: float32 [3072], P(('dp', 'ctx'))
- w_out_grad: float32 [1024, 1024], P(('dp', 'ctx'))
- b_out_grad: float32 [1024], P(('dp', 'ctx'))
- w_up_grad: float32 [1024, 4096], P(('dp', 'ctx'))
- b_up_grad: float32 [4096], P(('dp', 'ctx'))
- w_down_grad: float32 [4096, 1024], P(('dp', 'ctx'))
- b_down_grad: float32 [1024], P(('dp', 'ctx'))
- norm1_gain_grad: float32 [1024], P(('dp', 'ctx'))
- norm1_bias_grad: float32 [1024], P(('dp', 'ctx'))
- norm2_gain_grad: float32 [1024], P(('dp', 'ctx'))
- norm2_bias_grad: float32 [1024], P(('dp', 'ctx'))
Inputs may be any that keep to these rules, and one draw needn't show every extreme that they name: `segments`: in each sequence the ids never fall before a tail of one or more padding zeros; id 0 appears only there. Of the 2 sequences of each index of dp, one holds a document that starts within its first 128 tokens and ends within its last 128.
All inputs are finite; a program needn't handle non-finite values.
Results may differ from a plain program's by a relative error of at most 0.011.
Values may be sent and summed in bfloat16 or wider, within the bound.
A program may use at most 256 MiB of HBM per device.

v0:
```python
from functools import partial

import jax
import jax.numpy as jnp
from jax import lax
from jax.sharding import PartitionSpec as P

HEAD = 64
ROT = 16


def layer_norm(values, gain, shift):
    center = jnp.mean(values, axis=-1, keepdims=True)
    centered = values - center
    spread = jnp.mean(centered * centered, axis=-1, keepdims=True)
    return centered * lax.rsqrt(spread + 1e-05) * gain + shift


def rotary_tables(positions):
    half_rot = ROT // 2
    inverse = 10000.0 ** (-(2.0 * jnp.arange(half_rot, dtype=jnp.float32)) / ROT)
    angles = positions[:, None] * inverse[None, :]
    angles = jnp.concatenate([angles, angles], axis=-1)
    return (jnp.cos(angles)[:, None, :], jnp.sin(angles)[:, None, :])


def rotate(values, cosine, sine):
    half_rot = ROT // 2
    leading = values[..., :ROT]
    turned = jnp.concatenate([-leading[..., half_rot:], leading[..., :half_rot]], axis=-1)
    return jnp.concatenate([leading * cosine + turned * sine, values[..., ROT:]], axis=-1)


def allowed(query_pos, key_pos, query_docs, key_docs):
    same_doc = (key_docs[None, :] == query_docs[:, None]) & (query_docs[:, None] > 0)
    causal = key_pos[None, :] <= query_pos[:, None]
    return same_doc & causal | (key_pos[None, :] == query_pos[:, None])


def unpack(gathered):
    matrices = (gathered[0], gathered[2], gathered[4], gathered[6])
    vectors = tuple((gathered[index].astype(jnp.float32) for index in (1, 3, 5, 7, 8, 9, 10, 11)))
    return (matrices, vectors)


def per_device(
    tokens,
    cotangent,
    segments,
    w_qkv,
    b_qkv,
    w_out,
    b_out,
    w_up,
    b_up,
    w_down,
    b_down,
    norm1_gain,
    norm1_bias,
    norm2_gain,
    norm2_bias,
):
    shards = (
        w_qkv,
        b_qkv,
        w_out,
        b_out,
        w_up,
        b_up,
        w_down,
        b_down,
        norm1_gain,
        norm1_bias,
        norm2_gain,
        norm2_bias,
    )
    tok_rows = tokens.shape[0]
    micro_count = tokens.shape[1]
    model_width = tokens.shape[2]
    seq_len = segments.shape[1]
    head_count = model_width // HEAD
    score_scale = HEAD ** (-0.5)
    key_block = 512
    first_row = lax.axis_index("ctx") * tok_rows
    query_pos = first_row + jnp.arange(tok_rows, dtype=jnp.int32)
    key_pos = jnp.arange(seq_len, dtype=jnp.int32)
    cosine, sine = rotary_tables(query_pos.astype(jnp.float32))

    def turn(values):
        return rotate(values, cosine, sine)

    totals = None
    mixed_parts = []
    grad_parts = []
    for micro_step in range(micro_count):
        forward_set = (
            lax.all_gather(shards[0], ("dp", "ctx"), axis=0, tiled=True),
            lax.all_gather(shards[1], ("dp", "ctx"), axis=0, tiled=True),
            lax.all_gather(shards[2], ("dp", "ctx"), axis=0, tiled=True),
            lax.all_gather(shards[3], ("dp", "ctx"), axis=0, tiled=True),
            lax.all_gather(shards[4], ("dp", "ctx"), axis=0, tiled=True),
            lax.all_gather(shards[5], ("dp", "ctx"), axis=0, tiled=True),
            lax.all_gather(shards[6], ("dp", "ctx"), axis=0, tiled=True),
            lax.all_gather(shards[7], ("dp", "ctx"), axis=0, tiled=True),
            lax.all_gather(shards[8], ("dp", "ctx"), axis=0, tiled=True),
            lax.all_gather(shards[9], ("dp", "ctx"), axis=0, tiled=True),
            lax.all_gather(shards[10], ("dp", "ctx"), axis=0, tiled=True),
            lax.all_gather(shards[11], ("dp", "ctx"), axis=0, tiled=True),
        )
        matrices, vectors = unpack(forward_set)
        proj_qkv, proj_out, proj_up, proj_down = matrices
        bias_qkv, bias_out, bias_up, bias_down, gain_one, shift_one, gain_two, shift_two = vectors
        inputs_f = tokens[:, micro_step, :].astype(jnp.float32)
        doc_ids = segments[micro_step]
        query_docs = lax.dynamic_slice_in_dim(doc_ids, first_row, tok_rows, 0)
        normed_one = layer_norm(inputs_f, gain_one, shift_one).astype(jnp.bfloat16)
        normed_two = layer_norm(inputs_f, gain_two, shift_two).astype(jnp.bfloat16)
        joined = jnp.dot(normed_one, proj_qkv, preferred_element_type=jnp.float32) + bias_qkv
        queries = turn(joined[:, :model_width].reshape(tok_rows, head_count, HEAD)).astype(
            jnp.bfloat16
        )
        keys_rot = turn(
            joined[:, model_width : 2 * model_width].reshape(tok_rows, head_count, HEAD)
        ).astype(jnp.bfloat16)
        values_low = joined[:, 2 * model_width :].astype(jnp.bfloat16)
        keys_all, values_all = (
            lax.all_gather(keys_rot.reshape(tok_rows, model_width), "ctx", axis=0, tiled=True),
            lax.all_gather(values_low, "ctx", axis=0, tiled=True),
        )
        keys_all = keys_all.reshape(seq_len, head_count, HEAD)
        values_all = values_all.reshape(seq_len, head_count, HEAD)

        def block_scores(key_start):
            keys_part = keys_all[key_start : key_start + key_block]
            raw = (
                jnp.einsum("qhd,khd->hqk", queries, keys_part, preferred_element_type=jnp.float32)
                * score_scale
            )
            permitted = allowed(
                query_pos,
                key_pos[key_start : key_start + key_block],
                query_docs,
                doc_ids[key_start : key_start + key_block],
            )
            return (jnp.where(permitted[None], raw, -1e30), permitted)

        row_max = jnp.full((head_count, tok_rows), -1e30, jnp.float32)
        row_total = jnp.zeros((head_count, tok_rows), jnp.float32)
        kept_scores = []
        for key_start in range(0, seq_len, key_block):
            masked, permitted = block_scores(key_start)
            kept_scores.append(masked)
            new_max = jnp.maximum(row_max, jnp.max(masked, axis=-1))
            row_total = row_total * jnp.exp(row_max - new_max) + jnp.sum(
                jnp.exp(masked - new_max[..., None]), axis=-1
            )
            row_max = new_max
        log_total = row_max + jnp.log(row_total)
        context = jnp.zeros((tok_rows, head_count, HEAD), jnp.float32)
        for block_index, key_start in enumerate(range(0, seq_len, key_block)):
            probs = jnp.exp(kept_scores[block_index] - log_total[..., None]).astype(jnp.bfloat16)
            context = context + jnp.einsum(
                "hqk,khd->qhd",
                probs,
                values_all[key_start : key_start + key_block],
                preferred_element_type=jnp.float32,
            )
        context_low = context.reshape(tok_rows, model_width).astype(jnp.bfloat16)
        attention = jnp.dot(context_low, proj_out, preferred_element_type=jnp.float32) + bias_out
        act = jnp.dot(normed_two, proj_up, preferred_element_type=jnp.float32) + bias_up
        hidden = jax.nn.gelu(act, approximate=False).astype(jnp.bfloat16)
        feed = jnp.dot(hidden, proj_down, preferred_element_type=jnp.float32) + bias_down
        mixed_parts.append((inputs_f + attention + feed).astype(jnp.bfloat16))
        backward_set = (
            lax.all_gather(shards[0], ("dp", "ctx"), axis=0, tiled=True),
            lax.all_gather(shards[1], ("dp", "ctx"), axis=0, tiled=True),
            lax.all_gather(shards[2], ("dp", "ctx"), axis=0, tiled=True),
            lax.all_gather(shards[3], ("dp", "ctx"), axis=0, tiled=True),
            lax.all_gather(shards[4], ("dp", "ctx"), axis=0, tiled=True),
            lax.all_gather(shards[5], ("dp", "ctx"), axis=0, tiled=True),
            lax.all_gather(shards[6], ("dp", "ctx"), axis=0, tiled=True),
            lax.all_gather(shards[7], ("dp", "ctx"), axis=0, tiled=True),
            lax.all_gather(shards[8], ("dp", "ctx"), axis=0, tiled=True),
            lax.all_gather(shards[9], ("dp", "ctx"), axis=0, tiled=True),
            lax.all_gather(shards[10], ("dp", "ctx"), axis=0, tiled=True),
            lax.all_gather(shards[11], ("dp", "ctx"), axis=0, tiled=True),
        )
        matrices, vectors = unpack(backward_set)
        proj_qkv, proj_out, proj_up, proj_down = matrices
        gain_one, shift_one, gain_two, shift_two = vectors[4:]
        grad_low = cotangent[:, micro_step, :]
        grad_f = grad_low.astype(jnp.float32)
        bias_sum = jnp.sum(grad_f, axis=0)
        grad_down = jnp.dot(hidden.T, grad_low, preferred_element_type=jnp.float32)
        grad_out = jnp.dot(context_low.T, grad_low, preferred_element_type=jnp.float32)
        grad_hidden = jnp.dot(grad_low, proj_down.T, preferred_element_type=jnp.float32)
        _, gelu_pull = jax.vjp(partial(jax.nn.gelu, approximate=False), act)
        grad_act = gelu_pull(grad_hidden)[0].astype(jnp.bfloat16)
        grad_up = jnp.dot(normed_two.T, grad_act, preferred_element_type=jnp.float32)
        grad_bias_up = jnp.sum(grad_act.astype(jnp.float32), axis=0)
        grad_two = jnp.dot(grad_act, proj_up.T, preferred_element_type=jnp.float32)
        grad_context = (
            jnp.dot(grad_low, proj_out.T, preferred_element_type=jnp.float32)
            .reshape(tok_rows, head_count, HEAD)
            .astype(jnp.bfloat16)
        )
        row_delta = jnp.einsum("qhd,qhd->hq", grad_context.astype(jnp.float32), context)
        grad_queries = jnp.zeros((tok_rows, head_count, HEAD), jnp.float32)
        key_terms = []
        value_terms = []
        for key_start in range(0, seq_len, key_block):
            masked, permitted = block_scores(key_start)
            probs_f = jnp.where(permitted[None], jnp.exp(masked - log_total[..., None]), 0.0)
            probs = probs_f.astype(jnp.bfloat16)
            keys_part = keys_all[key_start : key_start + key_block]
            values_part = values_all[key_start : key_start + key_block]
            grad_probs = jnp.einsum(
                "qhd,khd->hqk", grad_context, values_part, preferred_element_type=jnp.float32
            )
            grad_scores = (probs_f * (grad_probs - row_delta[..., None])).astype(jnp.bfloat16)
            grad_queries = (
                grad_queries
                + jnp.einsum(
                    "hqk,khd->qhd", grad_scores, keys_part, preferred_element_type=jnp.float32
                )
                * score_scale
            )
            value_terms.append(
                jnp.einsum("hqk,qhd->khd", probs, grad_context, preferred_element_type=jnp.float32)
            )
            key_terms.append(
                jnp.einsum("hqk,qhd->khd", grad_scores, queries, preferred_element_type=jnp.float32)
                * score_scale
            )
        key_whole = jnp.concatenate(key_terms, axis=0).reshape(seq_len, model_width)
        value_whole = jnp.concatenate(value_terms, axis=0).reshape(seq_len, model_width)
        grad_keys, grad_values = (
            lax.psum_scatter(
                key_whole.astype(jnp.bfloat16), "ctx", scatter_dimension=0, tiled=True
            ).astype(jnp.float32),
            lax.psum_scatter(
                value_whole.astype(jnp.bfloat16), "ctx", scatter_dimension=0, tiled=True
            ).astype(jnp.float32),
        )
        _, turn_pull = jax.vjp(turn, jnp.zeros((tok_rows, head_count, HEAD), jnp.float32))
        grad_q_plain = turn_pull(grad_queries)[0].reshape(tok_rows, model_width)
        grad_k_plain = turn_pull(grad_keys.reshape(tok_rows, head_count, HEAD))[0].reshape(
            tok_rows, model_width
        )
        grad_joined = jnp.concatenate([grad_q_plain, grad_k_plain, grad_values], axis=1).astype(
            jnp.bfloat16
        )
        grad_qkv = jnp.dot(normed_one.T, grad_joined, preferred_element_type=jnp.float32)
        grad_bias_qkv = jnp.sum(grad_joined.astype(jnp.float32), axis=0)
        grad_one = jnp.dot(grad_joined, proj_qkv.T, preferred_element_type=jnp.float32)
        _, norm_pull_one = jax.vjp(layer_norm, inputs_f, gain_one, shift_one)
        input_one, grad_gain_one, grad_shift_one = norm_pull_one(grad_one)
        _, norm_pull_two = jax.vjp(layer_norm, inputs_f, gain_two, shift_two)
        input_two, grad_gain_two, grad_shift_two = norm_pull_two(grad_two)
        grad_parts.append((grad_f + input_one + input_two).astype(jnp.bfloat16))
        terms = (
            grad_qkv,
            grad_bias_qkv,
            grad_out,
            bias_sum,
            grad_up,
            grad_bias_up,
            grad_down,
            bias_sum,
            grad_gain_one,
            grad_shift_one,
            grad_gain_two,
            grad_shift_two,
        )
        if totals is None:
            totals = terms
        else:
            totals = tuple((total + term for total, term in zip(totals, terms)))
    owned = lax.psum_scatter(totals, ("dp", "ctx"), scatter_dimension=0, tiled=True)
    mixed_rows = jnp.stack(mixed_parts, axis=1)
    tokens_grad = jnp.stack(grad_parts, axis=1)
    return (
        mixed_rows,
        tokens_grad,
        owned[0],
        owned[1],
        owned[2],
        owned[3],
        owned[4],
        owned[5],
        owned[6],
        owned[7],
        owned[8],
        owned[9],
        owned[10],
        owned[11],
    )


def solution(mesh):
    placed = (
        P("ctx", "dp", None),
        P("ctx", "dp", None),
        P("dp", None),
        P(("dp", "ctx"), None),
        P(("dp", "ctx")),
        P(("dp", "ctx"), None),
        P(("dp", "ctx")),
        P(("dp", "ctx"), None),
        P(("dp", "ctx")),
        P(("dp", "ctx"), None),
        P(("dp", "ctx")),
        P(("dp", "ctx")),
        P(("dp", "ctx")),
        P(("dp", "ctx")),
        P(("dp", "ctx")),
    )
    return jax.shard_map(
        per_device,
        mesh=mesh,
        in_specs=placed,
        out_specs=(
            P("ctx", "dp", None),
            P("ctx", "dp", None),
            P(("dp", "ctx"), None),
            P(("dp", "ctx")),
            P(("dp", "ctx"), None),
            P(("dp", "ctx")),
            P(("dp", "ctx"), None),
            P(("dp", "ctx")),
            P(("dp", "ctx"), None),
            P(("dp", "ctx")),
            P(("dp", "ctx")),
            P(("dp", "ctx")),
            P(("dp", "ctx")),
            P(("dp", "ctx")),
        ),
        check_vma=False,
    )
```

profile of v0, /device:TPU:0, one launch (start us, length us, event | category | flops | bytes accessed | tf_op | source)
XLA Modules:
  0.0 1257.7 jit_solution(8316493526814080155)
XLA Ops:
  14.6 42.7 %all-reduce.31 = (bf16[1024]{0:T(1024)(128)(2,1)}, bf16[1024]{0:T(1024)(128)(2,1)}, bf16[1024]{0:T(1024)(128)(2,1)}, bf16[3072]{0:T(1024)(128)(2,1)S(1)}, bf16[1...) all-reduce(bf16[1024]{0:T(1024)(128)(2,1)S(1)} %dynamic-update-slic, ...), channel_id=1, replica_groups=mesh['dp'=4,'ctx'=8] {'dp','ctx'}, use_global_device_ids=true, to_apply=%add.22 | all-reduce | flops 9216 | bytes 36864
  57.3 2.3 fusion.228
  60.1 23.5 %all-gather.10.cloned.1.call-done = bf16[1024,3072]{1,0:T(8,128)(2,1)} async-done(((bf16[32,3072]{1,0:T(8,128)(2,1)}), bf16[1024,3072]{1,0:T(8,128)(2,1)}) %all-gather.10.cloned.1.call-update) | async-done | bytes 6291472 | tf_op jit(solution)/shard_map/all_gather | solution.py:97
  83.6 3.9 convolution_add_fusion.5
  88.5 3.9 convolution_add_fusion.6
  106.4 35.1 %all-gather.16.cloned.1.call-done = bf16[1024,1024]{1,0:T(8,128)(2,1)} async-done(((bf16[32,1024]{1,0:T(8,128)(2,1)}), bf16[1024,1024]{1,0:T(8,128)(2,1)}) %all-gather.16.cloned.1.call-update) | async-done | bytes 2097168 | tf_op jit(solution)/shard_map/all_gather | solution.py:99
  141.5 3.2 convolution_convert_fusion
  149.9 21.8 %all-gather.22.cloned.1.call-done = bf16[1024,1024]{1,0:T(8,128)(2,1)} async-done(((bf16[128,1024]{1,0:T(8,128)(2,1)}), bf16[1024,1024]{1,0:T(8,128)(2,1)}) %all-gather.22.cloned.1.call-update) | async-done | bytes 2097168 | tf_op jit(solution)/shard_map/all_gather | solution.py:128
  171.7 2.7 fusion.223
  174.4 2.3 copy.84
  178.1 23.7 %all-gather.12.cloned.1.call-done = bf16[1024,1024]{1,0:T(8,128)(2,1)} async-done(((bf16[128,1024]{1,0:T(8,128)(2,1)}), bf16[1024,1024]{1,0:T(8,128)(2,1)}) %all-gather.12.cloned.1.call-update) | async-done | bytes 2097168 | tf_op jit(solution)/shard_map/all_gather | solution.py:128
  201.8 2.7 fusion.221
  204.5 2.3 copy.79
  208.1 26.1 %all-gather.14.cloned.1.call-done = bf16[1024,1024]{0,1:T(8,128)(2,1)} async-done(((bf16[128,1024]{0,1:T(8,128)(2,1)}), bf16[1024,1024]{0,1:T(8,128)(2,1)}) %all-gather.14.cloned.1.call-update) | async-done | bytes 2097168 | tf_op jit(solution)/shard_map/all_gather | solution.py:127
  250.4 3.9 copy.103
  254.6 11.5 all-gather.24.cloned.1.call-done
  282.4 4.0 copy.107
  287.3 3.8 fusion.76
  294.2 4.0 copy.105
  298.8 3.8 fusion.78
  305.7 3.9 copy.109
  312.7 2.8 convolution_add_fusion.7
  316.0 2.6 fusion.235
  325.4 14.7 %reduce-scatter.29.cloned.1.call-done = bf16[128,1024]{1,0:T(8,128)(2,1)} async-done(((bf16[1024,1024]{1,0:T(8,128)(2,1)}), bf16[128,1024]{1,0:T(8,128)(2,1)}) %reduce-scatter.29.cloned.1.call-update) | async-done | bytes 262160
  342.8 34.2 %reduce-scatter.27.cloned.1.call-done = bf16[128,1024]{1,0:T(8,128)(2,1)} async-done(((bf16[1024,1024]{1,0:T(8,128)(2,1)}), bf16[128,1024]{1,0:T(8,128)(2,1)}) %reduce-scatter.27.cloned.1.call-update) | async-done | bytes 262160
  378.1 35.5 %reduce-scatter.31.cloned.1.call-done = bf16[128,1024]{1,0:T(8,128)(2,1)} async-done(((bf16[1024,1024]{1,0:T(8,128)(2,1)}), bf16[128,1024]{1,0:T(8,128)(2,1)}) %reduce-scatter.31.cloned.1.call-update) | async-done | bytes 262160
  419.5 6.5 convolution_add_fusion.2
  426.6 37.4 %all-gather = bf16[32,1,128]{2,1,0:T(2,128)(2,1)S(1)} all-gather(bf16[1,1,128]{2,1,0:T(2,128)(2,1)S(1)} %bitcast.365), channel_id=1, replica_groups=mesh['dp'=4,'ctx'=8] {'dp','ctx'}, dimensions={0}, use_global_device_ids=true | all-gather | bytes 8448 | tf_op jit(solution)/shard_map/all_gather | solution.py:102
  464.1 28.7 %all-gather.18.cloned.1.call-done = bf16[1024,4096]{1,0:T(8,128)(2,1)} async-done(((bf16[32,4096]{1,0:T(8,128)(2,1)}), bf16[1024,4096]{1,0:T(8,128)(2,1)}) %all-gather.18.cloned.1.call-update) | async-done | bytes 8388624 | tf_op jit(solution)/shard_map/all_gather | solution.py:101
  492.8 6.4 convolution_add_fusion.4
  499.2 2.7 convolution_add_fusion.3
  501.9 69.8 %all-gather.20.cloned.1.call-done = bf16[4096,1024]{1,0:T(8,128)(2,1)} async-done(((bf16[128,1024]{1,0:T(8,128)(2,1)}), bf16[4096,1024]{1,0:T(8,128)(2,1)}) %all-gather.20.cloned.1.call-update) | async-done | bytes 8388624 | tf_op jit(solution)/shard_map/all_gather | solution.py:103
  571.7 9.9 convert_reduce_fusion.1
  581.6 2.5 fusion.205
  585.6 7.6 convert_reduce_fusion
  593.2 8.3 convolution_add_fusion.1
  601.6 11.3 fusion.158
  612.9 13.7 %convolution_add_fusion = f32[4096,1024]{1,0:T(8,128)} fusion(f32[4096,1024]{1,0:T(8,128)} %fusion.158, bf16[128,1,1024]{2,0,1:T(8,128)(2,1)S(1)} %get-tuple-element.91, f32[128,4096]{1,0:T(8,128)S(1)} %copy-done.37), kind=kOutput, calls=%fused_computation | convolution fusion | flops 1112014848 | bytes 35913728 | tf_op jit(solution)/shard_map/dot_general | solution.py:194
  627.4 9.6 convolution_add_fusion.13
  637.6 8.4 convolution_add_fusion.12
  648.0 2.9 fusion.236
  650.9 2.9 fusion.238
  653.9 2.4 fusion.220
  661.5 40.5 %all-reduce.30 = (f32[3072]{0:T(1024)S(1)}, f32[1024]{0:T(1024)S(1)}, f32[4096]{0:T(1024)S(1)}, f32[1024]{0:T(1024)S(1)}, f32[1024]{0:T(1024)S(1)}, /*index=5*/f32[1024]{0:T(1024)S(1)}, f32[1024]{0:T(1024)S(1)}) all-reduce(f32[3072]{0:T(1024)S(1)} %add.382, f32[1024]{0:T(1024)S(1)} %add.384, ...), channel_id=7, replica_groups=mesh['dp'=4,'ctx'=8] {'dp','ctx'}, use_global_device_ids=true, to_apply=%region_27.28.clone | all-reduce | flops 12288 | bytes 98304
  708.4 7.4 reduce-scatter.19.cloned.1.call-done
  715.8 158.9 %reduce-scatter.17.cloned.1.call-done = f32[32,3072]{1,0:T(8,128)} async-done(((f32[1024,3072]{1,0:T(8,128)}), f32[32,3072]{1,0:T(8,128)}) %reduce-scatter.17.cloned.1.call-update) | async-done | bytes 393232 | tf_op jit(solution)/shard_map/reduce_scatter | solution.py:279
  874.7 188.6 %reduce-scatter.21.cloned.1.call-done = f32[32,4096]{1,0:T(8,128)} async-done(((f32[1024,4096]{1,0:T(8,128)}), f32[32,4096]{1,0:T(8,128)}) %reduce-scatter.21.cloned.1.call-update) | async-done | bytes 524304 | tf_op jit(solution)/shard_map/reduce_scatter | solution.py:279
  1063.3 187.2 %reduce-scatter.23.cloned.1.call-done = f32[128,1024]{1,0:T(8,128)} async-done(((f32[4096,1024]{1,0:T(8,128)}), f32[128,1024]{1,0:T(8,128)}) %reduce-scatter.23.cloned.1.call-update) | async-done | bytes 524304 | tf_op jit(solution)/shard_map/reduce_scatter | solution.py:279
  (388 shorter events, 107.6 us)
Async XLA Ops:
  7.2 76.4 %all-gather.10.cloned.1.call-start = ((), (), s32[]{:S(2)}) async-start(), calls=%async_computation.8 | async-start | bytes 6488064 | tf_op jit(solution)/shard_map/all_gather | solution.py:97
  7.9 133.6 %all-gather.16.cloned.1.call-start = ((), (), s32[]{:S(2)}) async-start(), calls=%async_computation.11 | async-start | bytes 2162688 | tf_op jit(solution)/shard_map/all_gather | solution.py:99
  8.7 163.0 %all-gather.22.cloned.1.call-start = ((), (), s32[]{:S(2)}) async-start(), calls=%async_computation.14 | async-start | bytes 2359296 | tf_op jit(solution)/shard_map/all_gather | solution.py:128
  57.3 362.2 %copy-start.43 = (f32[1024]{0:T(1024)}, f32[1024]{0:T(1024)S(1)}, u32[]{:S(2)}) copy-start(f32[1024]{0:T(1024)S(1)} %convert_element_type.205) | copy-start | bytes 12292
  60.0 27.4 %copy-start.80 = (f32[128]{0:T(128)}, f32[128]{0:T(128)S(1)}, u32[]{:S(2)}) copy-start(f32[128]{0:T(128)S(1)} %fusion.135) | copy-start | bytes 1540
  60.0 27.4 %copy-start.68 = (f32[128]{0:T(128)}, f32[128]{0:T(128)S(1)}, u32[]{:S(2)}) copy-start(f32[128]{0:T(128)S(1)} %fusion.173) | copy-start | bytes 1540
  88.2 113.5 %all-gather.12.cloned.1.call-start = ((), (), s32[]{:S(2)}) async-start(), calls=%async_computation.9 | async-start | bytes 2359296 | tf_op jit(solution)/shard_map/all_gather | solution.py:128
  94.4 139.7 %all-gather.14.cloned.1.call-start = ((), (), s32[]{:S(2)}) async-start(), calls=%async_computation.10 | async-start | bytes 2359296 | tf_op jit(solution)/shard_map/all_gather | solution.py:127
  95.1 6.2 copy-start.64
  95.1 6.2 copy-start.66
  98.7 5.1 copy-start.39
  98.9 5.6 copy-start.42
  103.7 162.4 %all-gather.24.cloned.1.call-start = ((), (), s32[]{:S(2)}) async-start(), calls=%async_computation.15 | async-start | bytes 2359296 | tf_op jit(solution)/shard_map/all_gather | solution.py:127
  105.9 205.1 %copy-start.21 = (bf16[128,1,1024]{2,0,1:T(8,128)(2,1)}, bf16[128,1,1024]{2,0,1:T(8,128)(2,1)S(1)}, u32[]{:S(2)}) copy-start(bf16[128,1,1024]{2,0,1:T(8,128)(2,1)S(1)} %get-tuple-element.93) | copy-start | bytes 786436
  106.3 137.7 %copy-start.61 = (pred[128,512]{1,0:T(8,128)(4,1)}, pred[128,512]{1,0:T(8,128)(4,1)S(1)}, u32[]{:S(2)}) copy-start(pred[128,512]{1,0:T(8,128)(4,1)S(1)} %get-tuple-element.172) | copy-start | bytes 196612
  106.4 140.1 %copy-start.59 = (pred[128,512]{1,0:T(8,128)(4,1)}, pred[128,512]{1,0:T(8,128)(4,1)S(1)}, u32[]{:S(2)}) copy-start(pred[128,512]{1,0:T(8,128)(4,1)S(1)} %get-tuple-element.169) | copy-start | bytes 196612
  145.4 101.0 %copy-start.50 = (bf16[128,16,64]{0,2,1:T(8,128)(2,1)}, bf16[128,16,64]{0,2,1:T(8,128)(2,1)S(1)}, u32[]{:S(2)}) copy-start(bf16[128,16,64]{0,2,1:T(8,128)(2,1)S(1)} %convolution_convert_fusion.1) | copy-start | bytes 786436
  149.4 173.2 %reduce-scatter.25.cloned.1.call-start = ((), (), s32[]{:S(2)}) async-start(), calls=%async_computation.20 | async-start | bytes 2359296
  236.7 7.3 copy-start.3
  237.7 8.7 copy-start.4
  240.2 6.2 copy-start.76
  254.4 85.7 %reduce-scatter.29.cloned.1.call-start = ((), (), s32[]{:S(2)}) async-start(), calls=%async_computation.22 | async-start | bytes 2359296
  268.7 7.4 copy-start.6
  269.6 8.8 copy-start.7
  272.2 6.3 copy-start.78
  286.5 90.5 %reduce-scatter.27.cloned.1.call-start = ((), (), s32[]{:S(2)}) async-start(), calls=%async_computation.21 | async-start | bytes 2359296
  298.2 115.5 %reduce-scatter.31.cloned.1.call-start = ((), (), s32[]{:S(2)}) async-start(), calls=%async_computation.23 | async-start | bytes 2359296
  309.6 183.2 %all-gather.18.cloned.1.call-start = ((), (), s32[]{:S(2)}) async-start(), calls=%async_computation.12 | async-start | bytes 8650752 | tf_op jit(solution)/shard_map/all_gather | solution.py:101
  310.4 261.3 %all-gather.20.cloned.1.call-start = ((), (), s32[]{:S(2)}) async-start(), calls=%async_computation.13 | async-start | bytes 8650752 | tf_op jit(solution)/shard_map/all_gather | solution.py:103
  311.0 404.8 %reduce-scatter.19.cloned.1.call-start = ((), (), s32[]{:S(2)}) async-start(), calls=%async_computation.17 | async-start | bytes 4325376 | tf_op jit(solution)/shard_map/reduce_scatter | solution.py:279
  315.5 559.1 %reduce-scatter.17.cloned.1.call-start = ((), (), s32[]{:S(2)}) async-start(), calls=%async_computation.16 | async-start | bytes 12976128 | tf_op jit(solution)/shard_map/reduce_scatter | solution.py:279
  324.6 90.2 %copy-start.67 = (f32[128,16]{0,1:T(8,128)S(1)}, f32[128,16]{0,1:T(8,128)}, u32[]{:S(2)}) copy-start(f32[128,16]{0,1:T(8,128)} %copy-done.66) | copy-start | bytes 24580
  342.1 73.9 %copy-start.65 = (f32[128,16]{0,1:T(8,128)S(1)}, f32[128,16]{0,1:T(8,128)}, u32[]{:S(2)}) copy-start(f32[128,16]{0,1:T(8,128)} %copy-done.64) | copy-start | bytes 24580
  378.1 39.3 %copy-start.34 = (bf16[128,1024]{0,1:T(8,128)(2,1)}, bf16[128,1024]{0,1:T(8,128)(2,1)S(1)}, u32[]{:S(2)}) copy-start(bf16[128,1024]{0,1:T(8,128)(2,1)S(1)} %copy.106) | copy-start | bytes 786436
  378.1 39.0 %copy-start.45 = (f32[128,16,48]{0,2,1:T(8,128)S(1)}, f32[128,16,48]{0,2,1:T(8,128)}, u32[]{:S(2)}) copy-start(f32[128,16,48]{0,2,1:T(8,128)} %split.64) | copy-start | bytes 1179652
  426.0 637.3 %reduce-scatter.21.cloned.1.call-start = ((), (), s32[]{:S(2)}) async-start(), calls=%async_computation.18 | async-start | bytes 17301504 | tf_op jit(solution)/shard_map/reduce_scatter | solution.py:279
  492.8 6.4 copy-start
  499.2 72.5 %copy-start.22 = (bf16[128,1,1024]{2,0,1:T(8,128)(2,1)S(1)}, bf16[128,1,1024]{2,0,1:T(8,128)(2,1)}, u32[]{:S(2)}) copy-start(bf16[128,1,1024]{2,0,1:T(8,128)(2,1)} %copy-done.21) | copy-start | bytes 786436
  601.6 648.9 %reduce-scatter.23.cloned.1.call-start = ((), (), s32[]{:S(2)}) async-start(), calls=%async_computation.19 | async-start | bytes 17301504 | tf_op jit(solution)/shard_map/reduce_scatter | solution.py:279
  601.6 11.3 copy-start.37
  627.4 9.6 copy-start.2
  627.4 9.6 copy-start.56
  627.4 10.2 copy-start.38
  637.1 10.9 slice-start
  637.6 8.4 copy-start.58
  637.6 10.3 slice-start.1
  647.9 5.8 slice-start.2
  702.1 548.9 %copy-start.91 = (f32[32]{0:T(128)}, f32[32]{0:T(128)S(1)}, u32[]{:S(2)}) copy-start(f32[32]{0:T(128)S(1)} %dynamic-slice.3) | copy-start | bytes 388
  (64 other events, 148.4 us)
Sparse Core Ops, SparseCore 0:
  11.0 72.4 all-gather.9
  86.5 54.9 all-gather.15
  143.7 27.9 all-gather.21
  173.1 28.5 all-gather.11
  203.8 30.3 all-gather.13
  236.2 29.8 all-gather.23
  268.4 34.9 reduce-scatter.24
  305.7 34.3 reduce-scatter.28
  342.4 34.5 reduce-scatter.26
  379.1 34.4 reduce-scatter.30
  416.6 76.1 all-gather.17
  495.7 75.9 all-gather.19
  574.5 141.2 reduce-scatter.18
  722.3 152.3 reduce-scatter.16
  877.5 185.7 reduce-scatter.20
  1066.1 184.3 reduce-scatter.22
where the time goes:
time: 1270 us; the launch traced here: 1260 us
  waiting for transfers between devices  869 us (68%)
  matrix products  151 us (12%)
  blocking collectives  121 us (10%)
  local copies, waits for them, and re-layouts  71.3 us (6%)
  other arithmetic  27.4 us (2%)
  between operations  16 us (1%)
    reduce_scatter x4, waiting for transfers between devices, per_device(): lax.psum_scatter(totals, ('dp', 'ctx'), scatter_dimension=0, tiled=True)  542 us
    unnamed x20, waiting for transfers between devices  87.2 us
    unnamed x2, blocking collectives  83.2 us
    all_gather x1, waiting for transfers between devices, per_device(): lax.all_gather(shards[6], ('dp', 'ctx'), axis=0, tiled=True)  69.8 us
    all_gather x2, waiting for transfers between devices, per_device(): lax.all_gather(values_low, 'ctx', axis=0, tiled=True)  45.5 us
    unnamed x224, local copies, waits for them, and re-layouts  40.1 us
    all_gather x2, waiting for transfers between devices, per_device(): lax.all_gather(keys_rot.reshape(tok_rows, model_width), 'ctx', axis=0, ti...  37.6 us
    all_gather x1, blocking collectives, per_device(): lax.all_gather(shards[5], ('dp', 'ctx'), axis=0, tiled=True)  37.4 us
  transfers between devices with their start and end apart: 16, of which 15 were waited for; matrix products, arithmetic and copies ran while one was open for 19% of the time, Pallas kernels for 0%

commit v1 on v0

v1 whole, which is shorter than its diff:
```python
from functools import partial

import jax
import jax.numpy as jnp
from jax import lax
from jax.experimental import pallas as pl
from jax.experimental.pallas import tpu as pltpu
from jax.sharding import PartitionSpec as P

HEAD = 64
ROT = 16
MIB = 1 << 20
MESH = pl.DeviceIdType.MESH
ANY = pl.BlockSpec(memory_space=pl.ANY)
F32 = jnp.float32
BF16 = jnp.bfloat16


class Place:
    def __init__(self, ndp, n):
        self.ndp, self.n, self.nz = ndp, n, n // 2
        self.dp = lax.axis_index("dp")
        self.c = lax.axis_index("ctx")
        self.z = self.c // 2
        self.core = lax.rem(self.c, 2)
        self.sib = self.c + 1 - 2 * self.core
        self.has_up = self.z + 1 < self.nz
        self.has_down = self.z > 0

    def barrier(self, ctx_all, dp_all):
        bar = pltpu.get_barrier_semaphore()
        count = 0
        if ctx_all:
            for j in range(1, self.n):
                peer = lax.rem(self.c + j, self.n)
                pl.semaphore_signal(bar, inc=1, device_id=(self.dp, peer), device_id_type=MESH)
                count += 1
        else:
            pl.semaphore_signal(bar, inc=1, device_id=(self.dp, self.sib), device_id_type=MESH)
            count += 1
            for ok, peer in ((self.has_up, self.c + 2), (self.has_down, self.c - 2)):

                @pl.when(ok)
                def _():
                    pl.semaphore_signal(bar, inc=1, device_id=(self.dp, peer), device_id_type=MESH)

        if dp_all:
            for j in range(1, self.ndp):
                peer = lax.rem(self.dp + j, self.ndp)
                pl.semaphore_signal(bar, inc=1, device_id=(peer, self.c), device_id_type=MESH)
                count += 1
        if not ctx_all:
            count = count + self.has_up.astype(jnp.int32) + self.has_down.astype(jnp.int32)
        pl.semaphore_wait(bar, count)


def remote(src, dst, send, recv, dp, c):
    return pltpu.make_async_remote_copy(
        src_ref=src,
        dst_ref=dst,
        send_sem=send,
        recv_sem=recv,
        device_id=(dp, c),
        device_id_type=MESH,
    )


class Gather:
    def __init__(self, at, src, dst, tok, sends, recvs):
        self.at, self.src, self.dst, self.tok, self.sends, self.recvs = at, src, dst, tok, sends, recvs

    def rows(self, c):
        return self.dst.at[:, pl.ds(pl.multiple_of(c * self.tok, self.tok), self.tok)]

    def copy(self, block, slot, c, src=None):
        at = self.at
        src = self.rows(block) if src is None else src
        return remote(src, self.rows(block), self.sends.at[slot], self.recvs.at[block], at.dp, c)

    def start(self):
        at = self.at

        @pl.when(at.has_up)
        def _():
            self.copy(at.c, 0, at.c + 2, self.src).start()

        @pl.when(at.has_down)
        def _():
            self.copy(at.c, 1, at.c - 2, self.src).start()

        self.copy(at.c, 2, at.sib, self.src).start()

    def step(self, k):
        at = self.at
        low, high = at.c - 2 * k, at.c + 2 * k

        @pl.when(at.z >= k)
        def _():
            self.copy(low, 0, at.c).wait_recv()

            @pl.when(at.has_up)
            def _():
                self.copy(low, 3 * k, at.c + 2).start()

            self.copy(low, 3 * k + 2, at.sib).start()

        @pl.when(at.z + k < at.nz)
        def _():
            self.copy(high, 0, at.c).wait_recv()

            @pl.when(at.has_down)
            def _():
                self.copy(high, 3 * k + 1, at.c - 2).start()

            self.copy(high, 3 * at.nz + k, at.sib).start()

    def finish(self):
        at = self.at
        for z in range(at.nz):
            self.copy(2 * z + 1 - at.core, 0, at.c).wait_recv()
        self.copy(at.c, 2, at.sib, self.src).wait_send()
        for k in range(at.nz):

            @pl.when((at.z >= k) & at.has_up)
            def _():
                self.copy(at.c, 3 * k, at.c).wait_send()

            @pl.when((at.z + k < at.nz) & at.has_down)
            def _():
                self.copy(at.c, 3 * k + 1, at.c).wait_send()

            if k:

                @pl.when(at.z >= k)
                def _():
                    self.copy(at.c, 3 * k + 2, at.c).wait_send()

                @pl.when(at.z + k < at.nz)
                def _():
                    self.copy(at.c, 3 * at.nz + k, at.c).wait_send()


def gather_slots(nz):
    return 4 * nz


class Exchange:
    def __init__(self, at, axis, src, dst, sends, recvs):
        self.at, self.axis, self.src, self.dst, self.sends, self.recvs = at, axis, src, dst, sends, recvs
        self.me, self.count = (at.c, at.n) if axis == "ctx" else (at.dp, at.ndp)

    def copy(self, peer, sender):
        at = self.at
        to = (at.dp, peer) if self.axis == "ctx" else (peer, at.c)
        return remote(self.src(peer), self.dst(sender), self.sends.at[peer], self.recvs.at[sender], *to)

    def start(self):
        for j in range(1, self.count):
            self.copy(lax.rem(self.me + j, self.count), self.me).start()

    def wait_recv(self):
        for j in range(1, self.count):
            peer = lax.rem(self.me + j, self.count)
            self.copy(peer, peer).wait_recv()

    def wait_send(self):
        for j in range(1, self.count):
            peer = lax.rem(self.me + j, self.count)
            self.copy(peer, self.me).wait_send()


def gather_kernel(ndp, n, tok_ref, cot_ref, wp_ref, wd_ref, wo_ref, vec_ref, x_out, g_out, w_out, wd_out, wo_out, vec_out, *sems):
    at = Place(ndp, n)
    tok = tok_ref.shape[1]
    (x_send, x_recv, g_send, g_recv, w1s, w1r, w2s, w2r, v1s, v1r, v2s, v2r, ds, dr, o1s, o1r, o2s, o2r, local) = sems
    at.barrier(True, True)
    own = (
        pltpu.make_async_copy(wp_ref.at[at.c], w_out.at[at.dp, at.c], local.at[0]),
        pltpu.make_async_copy(vec_ref, vec_out.at[at.dp, at.c], local.at[1]),
        pltpu.make_async_copy(wd_ref, wd_out.at[at.dp], local.at[2]),
        pltpu.make_async_copy(tok_ref, x_out.at[:, pl.ds(pl.multiple_of(at.c * tok, tok), tok)], local.at[3]),
        pltpu.make_async_copy(cot_ref, g_out.at[:, pl.ds(pl.multiple_of(at.c * tok, tok), tok)], local.at[4]),
    )
    for copy in own:
        copy.start()
    down_w = Exchange(at, "dp", lambda p: wd_ref, lambda s: wd_out.at[s], ds, dr)
    cols = Exchange(at, "ctx", lambda p: wp_ref.at[p], lambda s: w_out.at[at.dp, s], w1s, w1r)
    vecs = Exchange(at, "ctx", lambda p: vec_ref, lambda s: vec_out.at[at.dp, s], v1s, v1r)
    plane_w = Exchange(at, "dp", lambda p: w_out.at[at.dp], lambda s: w_out.at[s], w2s, w2r)
    plane_v = Exchange(at, "dp", lambda p: vec_out.at[at.dp], lambda s: vec_out.at[s], v2s, v2r)
    plane_o = Exchange(at, "dp", lambda p: wo_out, lambda s: wo_out, o2s, o2r)
    cols.start()
    vecs.start()
    index = at.dp * n + at.c
    heads_of, slot = index // ndp, lax.rem(index, ndp)

    def out_rows(b, c):
        return remote(wo_ref, wo_out.at[b], o1s, o1r.at[b], at.dp, c)

    @pl.when(heads_of != at.c)
    def _():
        out_rows(slot, heads_of).start()

    own_rows = pltpu.make_async_copy(wo_ref, wo_out.at[slot], local.at[5])

    @pl.when(heads_of == at.c)
    def _():
        own_rows.start()

    down_w.start()
    x_ag = Gather(at, tok_ref, x_out, tok, x_send, x_recv)
    g_ag = Gather(at, cot_ref, g_out, tok, g_send, g_recv)
    x_ag.start()
    own[0].wait()
    cols.wait_recv()
    plane_w.start()
    own[1].wait()
    vecs.wait_recv()
    plane_v.start()
    first = at.c * ndp // n

    @pl.when(at.dp == first)
    def _():
        for b in range(ndp):
            src = lax.rem(at.c * ndp + b, n)

            @pl.when(src != at.c)
            def _():
                out_rows(b, at.c).wait_recv()

            @pl.when(src == at.c)
            def _():
                own_rows.wait()

        plane_o.start()

    for k in range(1, at.nz):
        x_ag.step(k)
        if k == 1:
            g_ag.start()
    for k in range(1, at.nz):
        g_ag.step(k)
    x_ag.finish()
    g_ag.finish()

    @pl.when(heads_of != at.c)
    def _():
        out_rows(slot, heads_of).wait_send()

    @pl.when((heads_of == at.c) & (at.dp != first))
    def _():
        own_rows.wait()

    @pl.when(at.dp == first)
    def _():
        plane_o.wait_send()

    @pl.when(at.dp != first)
    def _():
        plane_o.copy(first, first).wait_recv()

    for copy in own[2:]:
        copy.wait()
    for part in (down_w, plane_w, plane_v):
        part.wait_recv()
    for part in (down_w, cols, vecs, plane_w, plane_v):
        part.wait_send()


def gather_all(ndp, n, tok, cot, wp, wd, wo, vec):
    mb, rows, width = tok.shape
    dma = pltpu.SemaphoreType.DMA
    slots = gather_slots(n // 2)
    return pl.pallas_call(
        partial(gather_kernel, ndp, n),
        out_shape=(
            jax.ShapeDtypeStruct((mb, rows * n, width), BF16),
            jax.ShapeDtypeStruct((mb, rows * n, width), BF16),
            jax.ShapeDtypeStruct((ndp,) + wp.shape, BF16),
            jax.ShapeDtypeStruct((ndp,) + wd.shape, BF16),
            jax.ShapeDtypeStruct((ndp,) + wo.shape, BF16),
            jax.ShapeDtypeStruct((ndp, n) + vec.shape, vec.dtype),
        ),
        in_specs=[ANY] * 6,
        out_specs=[ANY] * 6,
        scratch_shapes=[
            dma((slots,)), dma((n,)), dma((slots,)), dma((n,)),
            dma((n,)), dma((n,)), dma((ndp,)), dma((ndp,)),
            dma((n,)), dma((n,)), dma((ndp,)), dma((ndp,)),
            dma((ndp,)), dma((ndp,)),
            dma, dma((ndp,)), dma((ndp,)), dma((ndp,)),
            dma((6,)),
        ],
        compiler_params=pltpu.CompilerParams(collective_id=0, has_side_effects=True),
    )(tok, cot, wp, wd, wo, vec)


class Scatter:
    def __init__(self, at, part, out, sib_buf, low_buf, high_buf, stage, tok, sems):
        self.at, self.part, self.out, self.tok = at, part, out, tok
        self.sib_buf, self.low_buf, self.high_buf, self.stage = sib_buf, low_buf, high_buf, stage
        self.s_send, self.s_recv, self.up_send, self.up_recv, self.dn_send, self.dn_recv = sems

    def rows(self, c):
        return pl.ds(pl.multiple_of(c * self.tok, self.tok), self.tok)

    def cross(self, z):
        at = self.at
        src = self.part.at[:, self.rows(2 * z + 1 - at.core)]
        return remote(src, self.sib_buf.at[z], self.s_send.at[z], self.s_recv.at[z], at.dp, at.sib)

    def up(self, z):
        at = self.at
        return remote(self.stage.at[z], self.low_buf.at[z], self.up_send.at[z], self.up_recv.at[z], at.dp, at.c + 2)

    def down(self, z):
        at = self.at
        return remote(self.stage.at[z], self.high_buf.at[z], self.dn_send.at[z], self.dn_recv.at[z], at.dp, at.c - 2)

    def order(self):
        nz = self.at.nz
        for i in range(nz):
            yield nz - 1 - i
            if i != nz - 1 - i:
                pass

    def start(self):
        for i in range(self.at.nz):
            self.cross(i).start()

    def chip_sum(self, z):
        at = self.at
        mine = self.part[:, self.rows(2 * z + at.core)].astype(F32)
        return mine + self.sib_buf[z].astype(F32)

    def step(self, i):
        at = self.at
        up_z, dn_z = at.nz - 1 - i, i

        @pl.when(up_z > at.z)
        def _():
            self.cross(up_z).wait_recv()
            self.stage[up_z] = self.chip_sum(up_z).astype(BF16)

            @pl.when(at.has_down)
            def _():
                self.up(up_z).wait_recv()
                self.stage[up_z] = (self.stage[up_z].astype(F32) + self.low_buf[up_z].astype(F32)).astype(BF16)

            self.up(up_z).start()

        @pl.when(dn_z < at.z)
        def _():
            self.cross(dn_z).wait_recv()
            self.stage[dn_z] = self.chip_sum(dn_z).astype(BF16)

            @pl.when(at.has_up)
            def _():
                self.down(dn_z).wait_recv()
                self.stage[dn_z] = (self.stage[dn_z].astype(F32) + self.high_buf[dn_z].astype(F32)).astype(BF16)

            self.down(dn_z).start()

    def finish(self):
        at = self.at
        self.cross(at.z).wait_recv()
        self.out[...] = self.chip_sum(at.z)

        @pl.when(at.has_down)
        def _():
            self.up(at.z).wait_recv()
            self.out[...] += self.low_buf[at.z].astype(F32)

        @pl.when(at.has_up)
        def _():
            self.down(at.z).wait_recv()
            self.out[...] += self.high_buf[at.z].astype(F32)

        for z in range(at.nz):
            self.cross(z).wait_send()

            @pl.when(z > at.z)
            def _():
                self.up(z).wait_send()

            @pl.when(z < at.z)
            def _():
                self.down(z).wait_send()


def scatter_kernel(ndp, n, part_ref, out_ref, sib_buf, low_buf, high_buf, stage, *sems):
    at = Place(ndp, n)
    at.barrier(False, False)
    work = Scatter(at, part_ref, out_ref, sib_buf, low_buf, high_buf, stage, out_ref.shape[1], sems)
    work.start()
    for i in range(at.nz - 1):
        work.step(i)
    work.finish()


def scatter_ctx(ndp, n, part, collective):
    mb, seq, width = part.shape
    nz, tok = n // 2, seq // n
    dma = pltpu.SemaphoreType.DMA
    buf = pltpu.VMEM((nz, mb, tok, width), BF16)
    vmem = pl.BlockSpec(memory_space=pltpu.VMEM)
    return pl.pallas_call(
        partial(scatter_kernel, ndp, n),
        out_shape=jax.ShapeDtypeStruct((mb, tok, width), F32),
        in_specs=[vmem],
        out_specs=vmem,
        scratch_shapes=[buf, buf, buf, buf] + [dma((nz,))] * 6,
        compiler_params=pltpu.CompilerParams(collective_id=collective, has_side_effects=True, vmem_limit_bytes=48 * MIB),
    )(part)


def grads_kernel(ndp, n, wp_ref, wd_ref, wo_ref, v_ref, w_out, wd_out, wo_out, v_out, wbuf, wsum, dbuf, obuf, osum, vbuf, vsum, *sems):
    at = Place(ndp, n)
    (w1s, w1r, ds, dr, o1s, o1r, v1s, v1r, w2s, w2r, v2s, v2r, o2s, o2r, local) = sems
    at.barrier(True, True)
    first = at.c * ndp // n
    w1 = Exchange(at, "dp", lambda p: wp_ref.at[p], lambda s: wbuf.at[s], w1s, w1r)
    d1 = Exchange(at, "dp", lambda p: wd_ref.at[p], lambda s: dbuf.at[s], ds, dr)
    v1 = Exchange(at, "dp", lambda p: v_ref, lambda s: vbuf.at[s], v1s, v1r)
    o1 = Exchange(at, "dp", lambda p: wo_ref, lambda s: obuf.at[s], o1s, o1r)
    w1.start()
    v1.start()

    @pl.when(at.dp != first)
    def _():
        o1.copy(first, at.dp).start()

    d1.start()

    def total(ref, mine, get):
        ref[...] = mine
        for j in range(1, ndp):
            ref[...] += get(lax.rem(at.dp + j, ndp)).astype(F32)

    w1.wait_recv()
    total(wsum, wp_ref[at.dp].astype(F32), lambda s: wbuf[s])
    wbuf[at.dp] = wsum[...].astype(BF16)
    w2 = Exchange(at, "ctx", lambda p: wbuf.at[at.dp, p], lambda s: w_out.at[s], w2s, w2r)
    w2.start()
    w_out[at.c] = wbuf[at.dp, at.c]
    v1.wait_recv()
    total(vsum, v_ref[...], lambda s: vbuf[s])
    v2 = Exchange(at, "ctx", lambda p: vsum, lambda s: v_out.at[s], v2s, v2r)
    v2.start()
    v_out[at.c] = vsum[...]

    index = at.dp * n + at.c
    heads_of, slot = index // ndp, lax.rem(index, ndp)

    def out_rows(b, c):
        return remote(osum.at[b], wo_out, o2s.at[b], o2r, at.dp, c)

    @pl.when(at.dp == first)
    def _():
        o1.wait_recv()
        rows = wo_ref[...].astype(F32)
        for j in range(1, ndp):
            rows += obuf[lax.rem(at.dp + j, ndp)].astype(F32)
        osum[...] = rows.astype(BF16)
        for b in range(ndp):
            owner = lax.rem(at.c * ndp + b, n)

            @pl.when(owner != at.c)
            def _():
                out_rows(b, owner).start()

            @pl.when(owner == at.c)
            def _():
                wo_out[...] = osum[b]

    d1.wait_recv()
    total(wd_out, wd_ref[at.dp].astype(F32), lambda s: dbuf[s])

    @pl.when(heads_of != at.c)
    def _():
        out_rows(slot, at.c).wait_recv()

    w2.wait_recv()
    v2.wait_recv()
    for part in (w1, v1, d1, w2, v2):
        part.wait_send()

    @pl.when(at.dp != first)
    def _():
        o1.copy(first, at.dp).wait_send()

    @pl.when(at.dp == first)
    def _():
        for b in range(ndp):
            owner = lax.rem(at.c * ndp + b, n)

            @pl.when(owner != at.c)
            def _():
                out_rows(b, owner).wait_send()


def grads_all(ndp, n, wp, wd, wo, v):
    dma = pltpu.SemaphoreType.DMA
    vmem = pl.BlockSpec(memory_space=pltpu.VMEM)
    return pl.pallas_call(
        partial(grads_kernel, ndp, n),
        out_shape=(
            jax.ShapeDtypeStruct(wp.shape[1:], BF16),
            jax.ShapeDtypeStruct(wd.shape[1:], F32),
            jax.ShapeDtypeStruct(wo.shape[1:], BF16),
            jax.ShapeDtypeStruct((n,) + v.shape, F32),
        ),
        in_specs=[vmem] * 4,
        out_specs=[vmem] * 4,
        scratch_shapes=[
            pltpu.VMEM(wp.shape, BF16),
            pltpu.VMEM(wp.shape[1:], F32),
            pltpu.VMEM(wd.shape, BF16),
            pltpu.VMEM((ndp,) + wo.shape, BF16),
            pltpu.VMEM(wo.shape, BF16),
            pltpu.VMEM((ndp,) + v.shape, F32),
            pltpu.VMEM(v.shape, F32),
            dma((ndp,)), dma((ndp,)), dma((ndp,)), dma((ndp,)), dma((ndp,)), dma((ndp,)), dma((ndp,)), dma((ndp,)),
            dma((n,)), dma((n,)), dma((n,)), dma((n,)), dma((ndp,)), dma,
            dma((1,)),
        ],
        compiler_params=pltpu.CompilerParams(collective_id=3, has_side_effects=True, vmem_limit_bytes=48 * MIB),
    )(wp, wd, wo, v)


def rotary_tables(seq):
    half_rot = ROT // 2
    inverse = 10000.0 ** (-(2.0 * jnp.arange(half_rot, dtype=F32)) / ROT)
    angles = jnp.arange(seq, dtype=jnp.int32).astype(F32)[:, None] * inverse[None, :]
    angles = jnp.concatenate([angles, angles], axis=-1)
    return (jnp.cos(angles)[None, :, None, :], jnp.sin(angles)[None, :, None, :])


def rotate(values, cosine, sine, back=False):
    half_rot = ROT // 2
    lead = values[..., :ROT]
    if back:
        u = lead * sine
        turned = jnp.concatenate([u[..., half_rot:], -u[..., :half_rot]], axis=-1)
        return jnp.concatenate([lead * cosine + turned, values[..., ROT:]], axis=-1)
    turned = jnp.concatenate([-lead[..., half_rot:], lead[..., :half_rot]], axis=-1)
    return jnp.concatenate([lead * cosine + turned * sine, values[..., ROT:]], axis=-1)


def dot(a, b, dims=((1,), (0,))):
    return lax.dot_general(a, b, (dims, ((), ())), preferred_element_type=F32)


def per_device(ndp, n, tokens, cotangent, segments, w_qkv, b_qkv, w_out, b_out, w_up, b_up, w_down, b_down, g1, s1, g2, s2):
    tok, mb, width = tokens.shape
    seq = segments.shape[1]
    heads_all = width // HEAD
    hc = width // n
    heads = hc // HEAD
    rows_w = w_qkv.shape[0]
    rows_d = w_down.shape[0]
    fu = ndp * rows_d
    c = lax.axis_index("ctx")
    dp = lax.axis_index("dp")
    scale = HEAD ** (-0.5)

    cot = jnp.transpose(cotangent, (1, 0, 2))
    toks = jnp.transpose(tokens, (1, 0, 2))
    qkv_cols = w_qkv.reshape(rows_w, 3, n, hc).transpose(2, 0, 1, 3).reshape(n, rows_w, 3 * hc)
    up_cols = w_up.reshape(rows_w, ndp, n, rows_d).transpose(2, 0, 1, 3).reshape(n, rows_w, fu)
    wp = jnp.concatenate([qkv_cols, up_cols], axis=2)
    shard_vecs = (b_qkv, b_out, b_up, b_down, g1, s1, g2, s2)
    sizes = [v.shape[0] for v in shard_vecs]
    vec = jnp.concatenate(shard_vecs)
    lanes = 128
    per_vec = 16 * lanes
    vec = jnp.pad(vec, (0, per_vec - vec.shape[0])).reshape(16, lanes)
    x, g, w, wd, wo, vecs = gather_all(ndp, n, toks, cot, wp, w_down, w_out, vec)
    w = w.reshape(width, 3 * hc + fu)
    wq, wu = w[:, : 3 * hc], w[:, 3 * hc :]
    wd = wd.reshape(fu, width)
    wo = wo.reshape(hc, width)
    flat = vecs.reshape(ndp * n, per_vec).astype(F32)
    starts = [sum(sizes[:i]) for i in range(len(sizes))]
    full = [flat[:, s : s + z].reshape(-1) for s, z in zip(starts, sizes)]
    bq_all, bo, bu_all, bd, gain1, shift1, gain2, shift2 = full
    bq = lax.dynamic_index_in_dim(bq_all.reshape(3, n, hc), c, 1, keepdims=False).reshape(3 * hc)
    bu = lax.dynamic_index_in_dim(bu_all.reshape(ndp, n, rows_d), c, 1, keepdims=False).reshape(fu)

    xf = x.reshape(mb * seq, width).astype(F32)
    gl = g.reshape(mb * seq, width)
    mean = jnp.mean(xf, axis=-1, keepdims=True)
    cen = xf - mean
    rstd = lax.rsqrt(jnp.mean(cen * cen, axis=-1, keepdims=True) + 1e-05)
    normed = cen * rstd
    h1 = (normed * gain1 + shift1).astype(BF16)
    h2 = (normed * gain2 + shift2).astype(BF16)
    joined = (dot(h1, wq) + bq).reshape(mb, seq, 3, heads, HEAD)
    cosine, sine = rotary_tables(seq)
    q = rotate(joined[:, :, 0], cosine, sine).astype(BF16)
    k = rotate(joined[:, :, 1], cosine, sine).astype(BF16)
    v = joined[:, :, 2].astype(BF16)
    pos = jnp.arange(seq, dtype=jnp.int32)
    same = (segments[:, None, :] == segments[:, :, None]) & (segments[:, :, None] > 0)
    allow = (same & (pos[None, None, :] <= pos[None, :, None])) | (pos[None, None, :] == pos[None, :, None])
    scores = jnp.einsum("sqhd,skhd->shqk", q, k, preferred_element_type=F32) * scale
    scores = jnp.where(allow[:, None], scores, -1e30)
    top = jnp.max(scores, axis=-1, keepdims=True)
    e = jnp.exp(scores - top)
    probs = e / jnp.sum(e, axis=-1, keepdims=True)
    pl_low = probs.astype(BF16)
    ctx_f = jnp.einsum("shqk,skhd->sqhd", pl_low, v, preferred_element_type=F32)
    ctx = ctx_f.astype(BF16).reshape(mb * seq, hc)
    act = dot(h2, wu) + bu
    hidden = jax.nn.gelu(act, approximate=False).astype(BF16)
    part = (dot(ctx, wo) + dot(hidden, wd)).astype(BF16).reshape(mb, seq, width)
    mixed_sum = scatter_ctx(ndp, n, part, 1)
    mixed = (toks.astype(F32) + mixed_sum + bo + bd).astype(BF16)

    gf = gl.astype(F32)
    d_wd = dot(hidden, gl, ((0,), (0,)))
    d_wo = dot(ctx, gl, ((0,), (0,)))
    d_hidden = dot(gl, wd, ((1,), (1,)))
    _, pull = jax.vjp(partial(jax.nn.gelu, approximate=False), act)
    d_act = pull(d_hidden)[0].astype(BF16)
    d_wu = dot(h2, d_act, ((0,), (0,)))
    d_bu = jnp.sum(d_act.astype(F32), axis=0)
    d_h2 = dot(d_act, wu, ((1,), (1,)))
    d_ctx = dot(gl, wo, ((1,), (1,))).astype(BF16).reshape(mb, seq, heads, HEAD)
    d_probs = jnp.einsum("sqhd,skhd->shqk", d_ctx, v, preferred_element_type=F32)
    delta = jnp.sum(probs * d_probs, axis=-1, keepdims=True)
    d_scores = jnp.where(allow[:, None], probs * (d_probs - delta), 0.0).astype(BF16)
    d_q = jnp.einsum("shqk,skhd->sqhd", d_scores, k, preferred_element_type=F32) * scale
    d_k = jnp.einsum("shqk,sqhd->skhd", d_scores, q, preferred_element_type=F32) * scale
    d_v = jnp.einsum("shqk,sqhd->skhd", pl_low, d_ctx, preferred_element_type=F32)
    d_q = rotate(d_q, cosine, sine, True)
    d_k = rotate(d_k, cosine, sine, True)
    d_qkv = jnp.stack([d_q, d_k, d_v], axis=2).astype(BF16).reshape(mb * seq, 3 * hc)
    d_wq = dot(h1, d_qkv, ((0,), (0,)))
    d_bq = jnp.sum(d_qkv.astype(F32), axis=0)
    d_h1 = dot(d_qkv, wq, ((1,), (1,)))
    e_sum = (d_h1 * gain1 + d_h2 * gain2).astype(BF16).reshape(mb, seq, width)
    e_own = scatter_ctx(ndp, n, e_sum, 2)
    own_x = toks.astype(F32)
    o_mean = jnp.mean(own_x, axis=-1, keepdims=True)
    o_cen = own_x - o_mean
    o_rstd = lax.rsqrt(jnp.mean(o_cen * o_cen, axis=-1, keepdims=True) + 1e-05)
    o_n = o_cen * o_rstd
    t_grad = o_rstd * (e_own - jnp.mean(e_own, axis=-1, keepdims=True) - o_n * jnp.mean(e_own * o_n, axis=-1, keepdims=True))
    tokens_grad = (cot.astype(F32) + t_grad).astype(BF16)

    rows = [
        jnp.pad(d_bq, (0, width - 3 * hc)),
        jnp.pad(d_bu, (0, width - fu)),
        jnp.sum(d_h1 * normed, axis=0),
        jnp.sum(d_h1, axis=0),
        jnp.sum(d_h2 * normed, axis=0),
        jnp.sum(d_h2, axis=0),
        jnp.sum(gf, axis=0),
        jnp.zeros((width,), F32),
    ]
    dwp = jnp.concatenate([d_wq, d_wu], axis=1).astype(BF16).reshape(ndp, n, rows_w, 3 * hc + fu)
    dw, dwd, dwo, dv = grads_all(
        ndp, n, dwp, d_wd.astype(BF16).reshape(ndp, rows_d, width), d_wo.astype(BF16).reshape(ndp, rows_w, width), jnp.stack(rows)
    )
    index = dp * n + c
    g_qkv = dw[:, :, : 3 * hc].reshape(n, rows_w, 3, hc).transpose(1, 2, 0, 3).reshape(rows_w, 3 * width).astype(F32)
    g_up = dw[:, :, 3 * hc :].reshape(n, rows_w, ndp, rows_d).transpose(1, 2, 0, 3).reshape(rows_w, -1).astype(F32)
    g_bq = lax.dynamic_slice_in_dim(dv[:, 0, : 3 * hc].reshape(n, 3, hc).transpose(1, 0, 2).reshape(-1), index * sizes[0], sizes[0])
    own = lax.dynamic_index_in_dim(dv, c, 0, keepdims=False)
    g_bu = lax.dynamic_slice_in_dim(own[1], dp * rows_d, rows_d)
    four = lax.dynamic_slice_in_dim(jnp.sum(dv[:, 2:6], axis=0), index * rows_w, rows_w, axis=1)
    g_b = lax.dynamic_slice_in_dim(own[6], index * rows_w, rows_w)
    return (
        jnp.transpose(mixed, (1, 0, 2)),
        jnp.transpose(tokens_grad, (1, 0, 2)),
        g_qkv,
        g_bq,
        dwo.astype(F32),
        g_b,
        g_up,
        g_bu,
        dwd,
        g_b,
        four[0],
        four[1],
        four[2],
        four[3],
    )


def solution(mesh):
    every = ("dp", "ctx")
    mat, vec, act = P(every, None), P(every), P("ctx", "dp", None)
    placed = (act, act, P("dp", None), mat, vec, mat, vec, mat, vec, mat, vec, vec, vec, vec, vec)
    return jax.shard_map(
        partial(per_device, mesh.shape["dp"], mesh.shape["ctx"]),
        mesh=mesh,
        in_specs=placed,
        out_specs=(act, act, mat, vec, mat, vec, mat, vec, mat, vec, vec, vec, vec, vec),
        check_vma=False,
    )
```

time: 1270 us -> 482 us (0.38)
  waiting for transfers between devices: 869 us -> 0 us
  Pallas kernels: 0 us -> 254 us
  blocking collectives: 121 us -> 0 us
  matrix products: 151 us -> 133 us
  local copies, waits for them, and re-layouts: 71.3 us -> 55.6 us
  between operations: 16 us -> 1.88 us
    reduce_scatter x4 -> x0, waiting for transfers between devices: 542 us -> none  [per_device(): lax.psum_scatter(totals, ('dp', 'ctx'), scatter_dimension=0, tiled=True)]
    pallas_call x0 -> x4, Pallas kernels: none -> 254 us  [the longest x2 111 us: scatter_ctx(): pl.pallas_call(partial(scatter_kernel, ndp, n), out_shape=jax.ShapeDtypeS...]
    all_gather x8 -> x0, waiting for transfers between devices: 240 us -> none  [the longest x1 69.8 us: per_device(): lax.all_gather(shards[6], ('dp', 'ctx'), axis=0, tiled=True)]
    unnamed x20 -> x0, waiting for transfers between devices: 87.2 us -> none
    unnamed x2 -> x0, blocking collectives: 83.2 us -> none
    all_gather x1 -> x0, blocking collectives: 37.4 us -> none  [per_device(): lax.all_gather(shards[5], ('dp', 'ctx'), axis=0, tiled=True)]
    dot_general x48 -> x17, matrix products: 151 us -> 122 us  [the longest x12 51 us: dot(): return lax.dot_general(a, b, (dims, ((), ())), preferred_element_type=F32)]
    unnamed x224 -> x116, local copies, waits for them, and re-layouts: 40.1 us -> 18.4 us
  transfers between devices with their start and end apart: 16 -> 0, of which waited for: 15 -> 0; matrix products, arithmetic and copies ran while one was open for 19% -> 0% of each run, Pallas kernels for 0% -> 0%
where the time goes in v1:
time: 482 us; the launch traced here: 478 us
  Pallas kernels  254 us (53%)
  matrix products  133 us (28%)
  local copies, waits for them, and re-layouts  55.6 us (12%)
  other arithmetic  33.2 us (7%)
    pallas_call x2, Pallas kernels, scatter_ctx(): pl.pallas_call(partial(scatter_kernel, ndp, n), out_shape=jax.ShapeDtypeS...  111 us
    pallas_call x1, Pallas kernels, gather_all(): pl.pallas_call(partial(gather_kernel, ndp, n), out_shape=(jax.ShapeDtypeS...  91.8 us
    pallas_call x1, Pallas kernels, grads_all(): pl.pallas_call(partial(grads_kernel, ndp, n), out_shape=(jax.ShapeDtypeSt...  51.2 us
    dot_general x12, matrix products, dot(): return lax.dot_general(a, b, (dims, ((), ())), preferred_element_type=F32)  51 us
    dot_general x1, matrix products, per_device(): jnp.einsum('shqk,skhd->sqhd', d_scores, k, preferred_element_type=F32)  23.8 us
    dot_general x1, matrix products, per_device(): jnp.einsum('shqk,sqhd->skhd', d_scores, q, preferred_element_type=F32)  23.3 us
    unnamed x116, local copies, waits for them, and re-layouts  18.4 us
    dot_general x2, local copies, waits for them, and re-layouts, dot(): return lax.dot_general(a, b, (dims, ((), ())), preferred_element_type=F32)  13.1 us

profile of v1, /device:TPU:0, one launch (start us, length us, event | category | flops | bytes accessed | tf_op | source)
XLA Modules:
  0.0 478.1 jit_solution(13152900201286729775)
XLA Ops:
  0.7 1.0 copy.112
  4.1 2.0 copy.143
  7.7 91.8 %shard_map.254 = (bf16[2,1024,1024]{2,1,0:T(8,128)(2,1)}, bf16[2,1024,1024]{2,1,0:T(8,128)(2,1)}, bf16[4,8,32,896]{3,2,1,0:T(8,128)(2,1)}, bf16[4,128,1024]{2,1,...) custom-call(bf16[2,128,1024]{2,1,0:T(8,128)(2,1)} %bitcast.207, ...), custom_call_target="tpu_custom_call" | custom-call | tf_op jit(solution)/shard_map/pallas_call | solution.py:274
  99.5 5.4 %convert_reduce_fusion = (f32[1024]{0:T(1024)}, f32[2,1024]{1,0:T(2,128)S(1)}) fusion(bf16[2,1024,1024]{2,1,0:T(8,128)(2,1)} %get-tuple-element.29, bf16[2,1024,1024]{2,1,0:T(8,128)(2,1)} %get-tuple-element.24), kind=kLoop, calls=%fused_computation.10 | loop fusion | flops 8385536 | bytes 8400896 | tf_op jit(solution)/shard_map/reduce_sum | solution.py:659
  105.0 1.6 multiply_reduce_fusion.3
  108.3 6.1 %add_convert_fusion.4 = (bf16[2048,1024]{1,0:T(8,128)(2,1)}, bf16[2048,1024]{1,0:T(8,128)(2,1)}) fusion(bf16[2,1024,1024]{2,1,0:T(8,128)(2,1)} %get-tuple-element.24, f32[1024]{0:T(1024)S(1)} %add.142, f32[1024]{0:T(1024)S(1)} %mul.245, f32[2048]{0:T(1024)S(1)} %bitcast.230, f32[2048]{0:T(1024)S(1)} %bitcast.232, f32[1024]{0:T(1024)S(1)} %add.151, ...), kind=kLoop, calls=%fused_computation.20 | loop fusion | flops 18874368 | bytes 12615680 | tf_op jit(solution)/shard_map/convert_element_type | solution.py:596
  114.4 4.7 convolution_add_fusion
  119.2 5.4 %reshape.332 = f32[2,1024,3,2,64]{4,3,2,1,0:T(2,128)} reshape(f32[2048,384]{1,0:T(8,128)S(1)} %convolution_add_fusion) | data formatting | bytes 6291456 | tf_op jit(solution)/shard_map/reshape | solution.py:598
  124.6 3.8 fusion.109
  128.4 2.7 copy.109
  131.9 2.1 copy.110
  134.0 1.0 slice_negate_fusion.2
  135.2 1.9 fusion.87
  137.1 1.9 slice.230
  140.4 2.5 and_or_fusion
  143.0 10.8 %fusion.113 = (f32[2,2,1024]{2,1,0:T(2,128)S(1)}, f32[2,2,1024,1024]{2,3,1,0:T(8,128)}) fusion(pred[2,1024,1024]{1,2,0:T(8,128)(4,1)S(1)} %and_or_fusion, bf16[2,1024,2,48]{1,3,2,0:T(8,128)(2,1)S(1)} %copy-done.15, bf16[2,1024,2,16]{1,3,2,0:T(8,128)(2,1)} %get-tuple-element.111, bf16[2,1024,2,48]{1,3,2,0:T(8,128)(2,1)S(1)} %copy-done.13, ...), kind=kOutput, calls=%fused_computation.181 | convolution fusion | flops 555746304 | bytes 19939328 | tf_op jit(solution)/shard_map/sub | solution.py:609
  153.8 2.3 slice.169
  156.2 1.0 copy.108
  157.1 3.5 convolution_convert_fusion
  161.8 8.1 %fusion.81 = f32[2,2,1024,1024]{2,3,1,0:T(8,128)} fusion(bf16[2,1024,2,64]{1,3,2,0:T(8,128)(2,1)S(1)} %copy.83, bf16[2,1024,1,2,64]{1,4,3,0,2:T(8,128)(2,1)S(1)} %copy.108), kind=kOutput, calls=%fused_computation.104 | convolution fusion | flops 536870912 | bytes 17825792 | tf_op jit(solution)/shard_map/sqhd,skhd->shqk/dot_general | solution.py:630
  169.9 23.8 %fusion.47 = f32[2,1024,2,64]{1,3,2,0:T(8,128)} fusion(f32[2,2,1024,1024]{2,3,1,0:T(8,128)} %fusion.81, pred[2,1024,1024]{1,2,0:T(8,128)(4,1)} %copy-done.11, bf16[2,1024,2,48]{1,3,2,0:T(8,128)(2,1)S(1)} %copy-done.16, bf16[2,1024,2,16]{1,3,2,0:T(8,128)(2,1)S(1)} %copy-done.21, f32[2,2,1024,1024]{2,3,1,0:T(8,128)} %get-tuple-element.127, ...), kind=kOutput, calls=%fused_computation.70 | convolution fusion | flops 567546880 | bytes 37240832 | tf_op jit(solution)/shard_map/shqk,skhd->sqhd/dot_general | solution.py:633
  193.7 23.3 %fusion.44 = f32[2,1024,2,64]{1,3,2,0:T(8,128)S(1)} fusion(f32[2,2,1024,1024]{2,3,1,0:T(8,128)} %fusion.81, pred[2,1024,1024]{1,2,0:T(8,128)(4,1)} %copy-done.11, bf16[2,1024,2,48]{1,3,2,0:T(8,128)(2,1)S(1)} %copy-done.14, bf16[2,1024,2,16]{1,3,2,0:T(8,128)(2,1)S(1)} %copy-done.20, f32[2,2,1024,1024]{2,3,1,0:T(8,128)} %get-tuple-element.127, ...), kind=kOutput, calls=%fused_computation.69 | convolution fusion | flops 567546880 | bytes 37240832 | tf_op jit(solution)/shard_map/shqk,sqhd->skhd/dot_general | solution.py:634
  217.1 1.0 slice_multiply_fusion.3
  218.1 1.0 maximum_add_fusion
  219.1 1.2 slice.189
  220.5 8.4 %fusion.50 = bf16[2,1024,1,2,64]{1,4,3,0,2:T(8,128)(2,1)S(1)} fusion(bf16[2,1024,2,64]{1,3,2,0:T(8,128)(2,1)S(1)} %copy.83, f32[2,2,1024,1024]{2,3,1,0:T(8,128)} %get-tuple-element.127, f32[2,2,1024]{2,1,0:T(2,128)S(1)} %copy-done.47), kind=kOutput, calls=%fused_computation.71 | convolution fusion | flops 545259520 | bytes 17842176 | tf_op jit(solution)/shard_map/shqk,sqhd->skhd/dot_general | solution.py:635
  229.2 1.6 copy.88
  231.3 2.4 fusion.76
  233.8 2.3 fusion.74
  236.3 13.4 %convert_reduce_fusion.2 = (f32[512]{0:T(512)S(1)}, bf16[2048,512]{1,0:T(8,128)(2,1)S(1)}, f32[2048,512]{1,0:T(8,128)}) fusion(f32[2048,512]{1,0:T(8,128)S(1)} %fusion.74, f32[512]{0:T(512)S(1)} %bitcast.238, bf16[2048,1024]{1,0:T(8,128)(2,1)S(1)} %bitcast.190, bf16[512,1024]{1,0:T(8,128)(2,1)S(1)} %bitcast.246), kind=kOutput, calls=%fused_computation.29 | convolution fusion | flops 2226126336 | bytes 15732736 | tf_op jit(solution)/shard_map/dot_general | solution.py:551
  249.7 6.3 %fusion.105 = (f32[1024]{0:T(1024)S(1)}, f32[1024]{0:T(1024)S(1)}, bf16[2048,1024]{1,0:T(8,128)(2,1)}, f32[1024]{0:T(1024)S(1)}, f32[1024]{0:T(1024)S(1)}) fusion(f32[2048]{0:T(1024)S(1)} %bitcast.231, f32[2048]{0:T(1024)S(1)} %bitcast.233, bf16[2,1024,1024]{2,1,0:T(8,128)(2,1)S(1)} %copy-done.2, f32[1024]{0:T(1024)S(1)} %mul.260, ...), kind=kOutput, calls=%fused_computation.174 | convolution fusion | flops 2174742528 | bytes 19963904 | tf_op jit(solution)/shard_map/dot_general | solution.py:551
  256.2 4.7 add_convert_fusion
  260.9 6.5 %copy.89 = bf16[1024,2048]{1,0:T(8,128)(2,1)} copy(bf16[1024,2048]{0,1:T(8,128)(2,1)} %bitcast.188) | data formatting | bytes 8388608 | tf_op jit(solution)/shard_map/dot_general | solution.py:551
  267.4 4.5 fusion.41
  272.0 6.5 %copy.91 = bf16[1024,2048]{1,0:T(8,128)(2,1)} copy(bf16[1024,2048]{0,1:T(8,128)(2,1)} %bitcast.187) | data formatting | bytes 8388608 | tf_op jit(solution)/shard_map/dot_general | solution.py:551
  278.5 5.2 %fusion.32 = bf16[4,8,32,512]{3,2,1,0:T(8,128)(2,1)S(1)} fusion(bf16[4,8,32,2048]{3,2,1,0:T(8,128)(2,1)} %bitcast.199, bf16[2048,512]{1,0:T(8,128)(2,1)} %copy-done.45), kind=kOutput, calls=%fused_computation.64 | convolution fusion | flops 2148007936 | bytes 7340032 | tf_op jit(solution)/shard_map/dot_general | solution.py:551
  284.0 7.5 %fusion.58 = bf16[2,1024,2,64]{1,3,2,0:T(8,128)(2,1)S(1)} fusion(bf16[2,1024,1,2,64]{1,4,3,0,2:T(8,128)(2,1)S(1)} %copy.108, f32[2,2,1024,1024]{2,3,1,0:T(8,128)} %get-tuple-element.127, f32[2,2,1024]{2,1,0:T(2,128)S(1)} %copy-done.48), kind=kOutput, calls=%fused_computation.75 | convolution fusion | flops 545521664 | bytes 17842176 | tf_op jit(solution)/shard_map/shqk,skhd->sqhd/dot_general | solution.py:612
  293.8 1.2 multiply_convert_fusion
  295.0 2.3 convolution_convert_fusion.1
  297.4 51.2 %shard_map.257 = (bf16[8,32,896]{2,1,0:T(8,128)(2,1)S(1)}, f32[128,1024]{1,0:T(8,128)S(1)}, bf16[32,1024]{1,0:T(8,128)(2,1)S(1)}, f32[8,8,1024]{2,1,0:T(8,128)S(1)}) custom-call(bf16[4,8,32,896]{3,2,1,0:T(8,128)(2,1)S(1)} %pad_maximum_fusion.wp_ref, bf16[4,128,1024]{2,1,0:T(8,128)(2,1)S(1)} %bitcast.185, bf16[4,32,1024]{2,1,0:T(8,128)(2,1)S(1)} %bitcast.186, ...), custom_call_target="tpu_custom_call" | custom-call | tf_op jit(solution)/shard_map/pallas_call | solution.py:505
  349.1 1.1 copy.142
  354.1 4.3 fusion.114
  358.5 1.3 add_convert_fusion.2
  359.8 53.0 %shard_map.255 = f32[2,128,1024]{2,1,0:T(8,128)S(1)} custom-call(bf16[2,1024,1024]{2,1,0:T(8,128)(2,1)S(1)} %bitcast.183), custom_call_target="tpu_custom_call" | custom-call | tf_op jit(solution)/shard_map/pallas_call | solution.py:407
  412.8 58.5 %shard_map.256 = f32[2,128,1024]{2,1,0:T(8,128)S(1)} custom-call(bf16[2,1024,1024]{2,1,0:T(8,128)(2,1)S(1)} %bitcast.184), custom_call_target="tpu_custom_call" | custom-call | tf_op jit(solution)/shard_map/pallas_call | solution.py:407
  472.4 1.6 fusion.80
  473.9 1.3 copy.95
  475.2 1.3 copy.96
  (176 shorter events, 19.7 us)
Async XLA Ops:
  0.6 5.4 %copy-start.6 = (bf16[128,2,1024]{2,1,0:T(2,128)(2,1)S(1)}, bf16[128,2,1024]{2,1,0:T(2,128)(2,1)}, u32[]{:S(2)}) copy-start(bf16[128,2,1024]{2,1,0:T(2,128)(2,1)} %param.15) | copy-start | bytes 1572868
  0.7 6.3 %copy-start.35 = (bf16[96]{0:T(256)(128)(2,1)S(1)}, bf16[96]{0:T(256)(128)(2,1)}, u32[]{:S(2)}) copy-start(bf16[96]{0:T(256)(128)(2,1)} %param.19) | copy-start | bytes 580
  0.7 6.3 %copy-start.36 = (bf16[32]{0:T(256)(128)(2,1)S(1)}, bf16[32]{0:T(256)(128)(2,1)}, u32[]{:S(2)}) copy-start(bf16[32]{0:T(256)(128)(2,1)} %param.21) | copy-start | bytes 196
  0.7 6.3 %copy-start.37 = (bf16[128]{0:T(256)(128)(2,1)S(1)}, bf16[128]{0:T(256)(128)(2,1)}, u32[]{:S(2)}) copy-start(bf16[128]{0:T(256)(128)(2,1)} %param.23) | copy-start | bytes 772
  0.7 6.3 %copy-start.38 = (bf16[32]{0:T(256)(128)(2,1)S(1)}, bf16[32]{0:T(256)(128)(2,1)}, u32[]{:S(2)}) copy-start(bf16[32]{0:T(256)(128)(2,1)} %param.25) | copy-start | bytes 196
  0.7 6.2 %copy-start.39 = (bf16[32]{0:T(256)(128)(2,1)S(1)}, bf16[32]{0:T(256)(128)(2,1)}, u32[]{:S(2)}) copy-start(bf16[32]{0:T(256)(128)(2,1)} %param.26) | copy-start | bytes 196
  0.7 6.2 %copy-start.40 = (bf16[32]{0:T(256)(128)(2,1)S(1)}, bf16[32]{0:T(256)(128)(2,1)}, u32[]{:S(2)}) copy-start(bf16[32]{0:T(256)(128)(2,1)} %param.27) | copy-start | bytes 196
  0.7 6.2 %copy-start.41 = (bf16[32]{0:T(256)(128)(2,1)S(1)}, bf16[32]{0:T(256)(128)(2,1)}, u32[]{:S(2)}) copy-start(bf16[32]{0:T(256)(128)(2,1)} %param.28) | copy-start | bytes 196
  0.7 6.2 %copy-start.42 = (bf16[32]{0:T(256)(128)(2,1)S(1)}, bf16[32]{0:T(256)(128)(2,1)}, u32[]{:S(2)}) copy-start(bf16[32]{0:T(256)(128)(2,1)} %param.29) | copy-start | bytes 196
  99.5 5.5 %copy-start.1 = (bf16[2,1024,1024]{2,1,0:T(8,128)(2,1)S(1)}, bf16[2,1024,1024]{2,1,0:T(8,128)(2,1)}, u32[]{:S(2)}) copy-start(bf16[2,1024,1024]{2,1,0:T(8,128)(2,1)} %get-tuple-element.24) | copy-start | bytes 12582916
  104.9 2.3 copy-start.22
  107.2 7.2 %copy-start.30 = (f32[1,8,2,128]{3,1,2,0:T(8,128)}, f32[1,8,2,128]{3,1,2,0:T(8,128)S(1)}, u32[]{:S(2)}) copy-start(f32[1,8,2,128]{3,1,2,0:T(8,128)S(1)} %copy.150) | copy-start | bytes 24580
  107.2 7.2 %copy-start.32 = (f32[1,8,2,128]{3,1,2,0:T(8,128)}, f32[1,8,2,128]{3,1,2,0:T(8,128)S(1)}, u32[]{:S(2)}) copy-start(f32[1,8,2,128]{3,1,2,0:T(8,128)S(1)} %copy.151) | copy-start | bytes 24580
  108.1 6.2 %copy-start.27 = (f32[1024]{0:T(1024)}, f32[1024]{0:T(1024)S(1)}, u32[]{:S(2)}) copy-start(f32[1024]{0:T(1024)S(1)} %add.142) | copy-start | bytes 12292
  131.9 8.6 %copy-start.24 = (s32[2,1024]{1,0:T(2,128)S(1)}, s32[2,1024]{1,0:T(2,128)}, u32[]{:S(2)}) copy-start(s32[2,1024]{1,0:T(2,128)} %param.17) | copy-start | bytes 24580
  139.8 3.2 copy-start.13
  139.8 3.2 copy-start.15
  139.8 3.2 copy-start.20
  143.0 10.8 %copy-start.11 = (pred[2,1024,1024]{1,2,0:T(8,128)(4,1)}, pred[2,1024,1024]{1,2,0:T(8,128)(4,1)S(1)}, u32[]{:S(2)}) copy-start(pred[2,1024,1024]{1,2,0:T(8,128)(4,1)S(1)} %and_or_fusion) | copy-start | bytes 6291460
  153.8 39.9 %copy-start.46 = (f32[2,2,1024]{2,1,0:T(2,128)}, f32[2,2,1024]{2,1,0:T(2,128)S(1)}, u32[]{:S(2)}) copy-start(f32[2,2,1024]{2,1,0:T(2,128)S(1)} %get-tuple-element.126) | copy-start | bytes 49156
  161.8 8.1 %copy-start.16 = (bf16[2,1024,2,48]{1,3,2,0:T(8,128)(2,1)S(1)}, bf16[2,1024,2,48]{1,3,2,0:T(8,128)(2,1)}, u32[]{:S(2)}) copy-start(bf16[2,1024,2,48]{1,3,2,0:T(8,128)(2,1)} %slice.230) | copy-start | bytes 1179652
  161.8 8.1 %copy-start.21 = (bf16[2,1024,2,16]{1,3,2,0:T(8,128)(2,1)S(1)}, bf16[2,1024,2,16]{1,3,2,0:T(8,128)(2,1)}, u32[]{:S(2)}) copy-start(bf16[2,1024,2,16]{1,3,2,0:T(8,128)(2,1)} %get-tuple-element.111) | copy-start | bytes 393220
  169.9 23.8 %copy-start.14 = (bf16[2,1024,2,48]{1,3,2,0:T(8,128)(2,1)S(1)}, bf16[2,1024,2,48]{1,3,2,0:T(8,128)(2,1)}, u32[]{:S(2)}) copy-start(bf16[2,1024,2,48]{1,3,2,0:T(8,128)(2,1)} %slice.231) | copy-start | bytes 1179652
  217.0 3.4 copy-start.47
  228.9 2.4 copy-start.17
  231.3 2.5 copy-start.3
  233.8 2.4 copy-start.4
  233.8 2.5 copy-start.44
  236.2 13.5 %copy-start.8 = (f32[2048,512]{1,0:T(8,128)}, f32[2048,512]{1,0:T(8,128)S(1)}, u32[]{:S(2)}) copy-start(f32[2048,512]{1,0:T(8,128)S(1)} %fusion.74) | copy-start | bytes 12582916
  236.3 13.4 %copy-start.2 = (bf16[2,1024,1024]{2,1,0:T(8,128)(2,1)S(1)}, bf16[2,1024,1024]{2,1,0:T(8,128)(2,1)}, u32[]{:S(2)}) copy-start(bf16[2,1024,1024]{2,1,0:T(8,128)(2,1)} %get-tuple-element.24) | copy-start | bytes 12582916
  236.3 13.4 %copy-start.31 = (f32[1,8,2,128]{3,1,2,0:T(8,128)S(1)}, f32[1,8,2,128]{3,1,2,0:T(8,128)}, u32[]{:S(2)}) copy-start(f32[1,8,2,128]{3,1,2,0:T(8,128)} %copy-done.30) | copy-start | bytes 24580
  236.3 13.4 %copy-start.33 = (f32[1,8,2,128]{3,1,2,0:T(8,128)S(1)}, f32[1,8,2,128]{3,1,2,0:T(8,128)}, u32[]{:S(2)}) copy-start(f32[1,8,2,128]{3,1,2,0:T(8,128)} %copy-done.32) | copy-start | bytes 24580
  249.6 6.3 %copy-start.45 = (bf16[2048,512]{1,0:T(8,128)(2,1)}, bf16[2048,512]{1,0:T(8,128)(2,1)S(1)}, u32[]{:S(2)}) copy-start(bf16[2048,512]{1,0:T(8,128)(2,1)S(1)} %get-tuple-element.83) | copy-start | bytes 6291460
  249.7 6.4 %copy-start.34 = (f32[1024]{0:T(1024)S(1)}, f32[1024]{0:T(1024)}, u32[]{:S(2)}) copy-start(f32[1024]{0:T(1024)} %get-tuple-element.128) | copy-start | bytes 12292
  249.7 6.5 %copy-start.23 = (f32[2,1024]{1,0:T(2,128)S(1)}, f32[2,1024]{1,0:T(2,128)}, u32[]{:S(2)}) copy-start(f32[2,1024]{1,0:T(2,128)} %copy-done.22) | copy-start | bytes 24580
  249.7 6.5 %copy-start.28 = (f32[1024]{0:T(1024)S(1)}, f32[1024]{0:T(1024)}, u32[]{:S(2)}) copy-start(f32[1024]{0:T(1024)} %copy-done.27) | copy-start | bytes 12292
  249.7 6.5 %copy-start.29 = (f32[2,1024]{1,0:T(2,128)S(1)}, f32[2,1024]{1,0:T(2,128)}, u32[]{:S(2)}) copy-start(f32[2,1024]{1,0:T(2,128)} %get-tuple-element.118) | copy-start | bytes 24580
  278.5 5.4 %copy-start.48 = (f32[2,2,1024]{2,1,0:T(2,128)S(1)}, f32[2,2,1024]{2,1,0:T(2,128)}, u32[]{:S(2)}) copy-start(f32[2,2,1024]{2,1,0:T(2,128)} %copy-done.46) | copy-start | bytes 49156
  284.0 8.2 %copy-start.5 = (bf16[2,1024,1024]{2,1,0:T(8,128)(2,1)S(1)}, bf16[2,1024,1024]{2,1,0:T(8,128)(2,1)}, u32[]{:S(2)}) copy-start(bf16[2,1024,1024]{2,1,0:T(8,128)(2,1)} %get-tuple-element.29) | copy-start | bytes 12582916
  284.0 8.9 %copy-start.10 = (f32[2048,512]{1,0:T(8,128)S(1)}, f32[2048,512]{1,0:T(8,128)}, u32[]{:S(2)}) copy-start(f32[2048,512]{1,0:T(8,128)} %get-tuple-element.84) | copy-start | bytes 12582916
  291.5 2.4 copy-start.9
  295.0 2.4 copy-start.12
  353.5 123.1 %copy-start.43 = (f32[32]{0:T(128)}, f32[32]{0:T(128)S(1)}, u32[]{:S(2)}) copy-start(f32[32]{0:T(128)S(1)} %dynamic-slice_bitcast_fusion.1) | copy-start | bytes 388
  354.1 4.4 copy-start.18
  359.8 53.0 %copy-start = (bf16[2048,1024]{1,0:T(8,128)(2,1)S(1)}, bf16[2048,1024]{1,0:T(8,128)(2,1)}, u32[]{:S(2)}) copy-start(bf16[2048,1024]{1,0:T(8,128)(2,1)} %get-tuple-element.87) | copy-start | bytes 12582916
  359.8 111.6 %copy-start.7 = (bf16[128,2,1024]{2,1,0:T(2,128)(2,1)S(1)}, bf16[128,2,1024]{2,1,0:T(2,128)(2,1)}, u32[]{:S(2)}) copy-start(bf16[128,2,1024]{2,1,0:T(2,128)(2,1)} %param.15) | copy-start | bytes 1572868
  412.8 59.4 %copy-start.26 = (f32[32,32]{1,0:T(8,128)S(1)}, f32[32,32]{1,0:T(8,128)}, u32[]{:S(2)}) copy-start(f32[32,32]{1,0:T(8,128)} %get-tuple-element.104) | copy-start | bytes 12292
  412.8 59.5 %copy-start.25 = (f32[32,32]{1,0:T(8,128)S(1)}, f32[32,32]{1,0:T(8,128)}, u32[]{:S(2)}) copy-start(f32[32,32]{1,0:T(8,128)} %get-tuple-element.105) | copy-start | bytes 12292
  (1 other events, 2.2 us)
